TPU v7x, 32 devices: a whole 2x2x4 slice. The times are simulated.
32 devices in a mesh: groups: 2 (over x), hits: 8 (over z, y), heads: 2 (over core).
Axes of the slice: x: 2, y: 2, z: 4, core: 2. Of those that a mesh axis runs over, the one named last changes fastest.
Arguments:
- queries: bfloat16 [2048, 2048], P('groups', 'heads'), parts along dimension 0, may hold values from -13.5 to 13.5
- keys: bfloat16 [8192, 2048], P(('groups', 'hits'), 'heads'), parts along dimension 0, may hold values from -36 to 36
- values: bfloat16 [8192, 2048], P(('groups', 'hits'), 'heads'), parts along dimension 0, may hold values from -6 to 6
- hit_counts: int32 [16], P(('groups', 'hits')), parts along dimension 0, may hold values from 128 to 512, as said below
- latents: bfloat16 [2048, 2048], P(('groups', 'hits'), 'heads'), parts along dimension 0, may hold values from -23 to 23
- out_proj: bfloat16 [2048, 2048], P('heads'), may hold values from -1 to 1
- norm_gain: float32 [2048], P('heads'), may hold values from 0.1 to 1.9
- up_proj: bfloat16 [2048, 8192], P('heads', 'hits'), may hold values from -0.125 to 0.125
- down_proj: bfloat16 [8192, 2048], P('hits', 'heads'), may hold values from -0.25 to 0.25
Outputs:
- mixed: bfloat16 [2048, 2048], P(('groups', 'hits'), 'heads'), parts along dimension 0
There are 2 independent parts, one for each index of `groups`. A program takes and returns all parts, laid end to end along the dimension named above; an argument that names none is the same for every part. Nothing has to cross between parts.
Inputs may be any that keep to these rules, and one draw needn't show every extreme that they name: hit_counts[s] live hits fill the first slots of shard s; some shard is full and some holds exactly 128.
All inputs are finite; a program needn't handle non-finite values.
Results may differ from a plain program's by a relative error of at most 0.012.
Values may be sent and summed in bfloat16 or wider, within the bound.
A program may use at most 64 MiB of HBM per device.

v0:
```python
import math

import jax
import jax.numpy as jnp
from jax import lax
from jax.sharding import PartitionSpec as P

D = 2048
HD = 128


def shards(queries, keys, values, hit_counts, latents, out_proj, norm_gain, up_proj, down_proj):
    width = keys.shape[1]
    local_heads = width // HD
    score_scale = 1.0 / math.sqrt(HD)
    live_mask = lax.broadcasted_iota(jnp.int32, (1, keys.shape[0]), 1) < hit_counts[0]

    def merged(row_top, row_total, context):
        row_best = lax.pmax(row_top, "hits")
        factor = jnp.exp(row_top - row_best)
        total_sum, context_sum = (
            lax.psum_scatter(row_total * factor, "hits", scatter_dimension=1, tiled=True),
            lax.psum_scatter(context * factor[..., None], "hits", scatter_dimension=1, tiled=True),
        )
        return (context_sum / total_sum[..., None]).astype(jnp.bfloat16)

    def one_head(head_index):
        col_start = head_index * HD
        q_head = lax.dynamic_slice_in_dim(queries, col_start, HD, 1)
        k_head = lax.dynamic_slice_in_dim(keys, col_start, HD, 1)
        v_head = lax.dynamic_slice_in_dim(values, col_start, HD, 1)
        scores = (
            lax.dot_general(
                q_head, k_head, (((1,), (1,)), ((), ())), preferred_element_type=jnp.float32
            )
            * score_scale
        )
        scores = jnp.where(live_mask, scores, -1e30)
        row_top = jnp.max(scores, axis=1)
        weights = jnp.where(live_mask, jnp.exp(scores - row_top[:, None]), 0.0)
        row_total = jnp.sum(weights, axis=1)
        context = jnp.dot(weights.astype(jnp.bfloat16), v_head, preferred_element_type=jnp.float32)
        return (row_top, row_total, context)

    context = merged(*lax.map(one_head, jnp.arange(local_heads, dtype=jnp.int32)))
    weights_out = out_proj.reshape(local_heads, HD, out_proj.shape[1])
    projected = jnp.einsum("hrd,hde->re", context, weights_out, preferred_element_type=jnp.float32)
    attended = lax.psum_scatter(projected, "heads", scatter_dimension=1, tiled=True)
    stream = latents.astype(jnp.float32) + attended
    squares = lax.psum(jnp.sum(stream * stream, axis=1), "heads")
    normed = (stream * lax.rsqrt(squares / D + 1e-06)[:, None] * norm_gain[None, :]).astype(
        jnp.bfloat16
    )
    partial_units = jnp.dot(
        lax.all_gather(normed, "hits", axis=0, tiled=True),
        up_proj,
        preferred_element_type=jnp.float32,
    )
    summed_units = lax.psum(partial_units, "heads")
    hidden = jax.nn.gelu(summed_units).astype(jnp.bfloat16)
    branch_out = lax.psum_scatter(
        jnp.dot(hidden, down_proj, preferred_element_type=jnp.float32),
        "hits",
        scatter_dimension=0,
        tiled=True,
    )
    return (stream + branch_out).astype(jnp.bfloat16)


def solution(mesh):
    return jax.shard_map(
        shards,
        mesh=mesh,
        in_specs=(
            P("groups", "heads"),
            P(("groups", "hits"), "heads"),
            P(("groups", "hits"), "heads"),
            P(("groups", "hits")),
            P(("groups", "hits"), "heads"),
            P("heads", None),
            P("heads"),
            P("heads", "hits"),
            P("hits", "heads"),
        ),
        out_specs=P(("groups", "hits"), "heads"),
        check_vma=False,
    )
```

profile of v0, /device:TPU:0, one launch (start us, length us, event | category | flops | bytes accessed | tf_op | source)
XLA Modules:
  0.0 450.3 jit_solution(14915383482989247984)
XLA Ops:
  6.5 54.9 %while.15 = (s32[]{:T(128)}, f32[8,1024]{1,0:T(8,128)S(1)}, f32[8,1024]{1,0:T(8,128)S(1)}, f32[8,1024,128]{2,1,0:T(8,128)}, s32[8]{0:T(128)S(1)}, /*index=5*/bf1...) while((s32[]{:T(128)}, f32[8,1024]{1,0:T(8,128)S(1)}, ...), condition=%wide.region_3.4_spmd.clone, body=%wide.region_0.3_spmd.clone.sunk | while | flops 275249664 | bytes 7376583 | solution.py:45
  6.6 0.7 dynamic_slice.34
  7.9 0.7 compare_reduce_fusion.2
  8.6 1.4 fusion.52
  10.1 2.5 fusion.54
  13.4 0.7 dynamic_slice.34
  14.8 0.7 compare_reduce_fusion.2
  15.4 1.4 fusion.52
  16.9 2.6 fusion.54
  20.3 0.7 dynamic_slice.34
  21.6 0.7 compare_reduce_fusion.2
  22.3 1.4 fusion.52
  23.8 2.6 fusion.54
  27.1 0.7 dynamic_slice.34
  28.5 0.7 compare_reduce_fusion.2
  29.2 1.5 fusion.52
  30.6 2.6 fusion.54
  34.0 0.7 dynamic_slice.34
  35.4 0.7 compare_reduce_fusion.2
  36.1 1.4 fusion.52
  37.5 2.6 fusion.54
  40.9 0.7 dynamic_slice.34
  42.2 0.7 compare_reduce_fusion.2
  42.9 1.4 fusion.52
  44.4 2.6 fusion.54
  47.8 0.7 dynamic_slice.34
  49.1 0.7 compare_reduce_fusion.2
  49.8 1.5 fusion.52
  51.3 2.5 fusion.54
  54.6 0.7 dynamic_slice.34
  56.0 0.7 compare_reduce_fusion.2
  56.6 1.4 fusion.52
  58.1 2.6 fusion.54
  61.5 38.8 %pmax.7 = f32[8,1024]{1,0:T(8,128)S(1)} all-reduce(f32[8,1024]{1,0:T(8,128)S(1)} %get-tuple-element.55), channel_id=1, replica_groups=mesh['groups'=2,'hits'=8,'heads'=2] {'hits'}, use_global_device_ids=true, to_apply=%region_4.5 | all-reduce | flops 8192 | bytes 65536 | tf_op jit(solution)/shard_map/pmax | solution.py:19
  101.0 4.2 broadcast_multiply_fusion
  105.3 46.7 %reduce-scatter.7.cloned.1.call-done = f32[8,128]{1,0:T(8,128)} async-done(((f32[8,1024]{1,0:T(8,128)}), f32[8,128]{1,0:T(8,128)}) %reduce-scatter.7.cloned.1.call-update) | async-done | bytes 4112 | tf_op jit(solution)/shard_map/reduce_scatter | solution.py:22
  152.0 90.6 %reduce-scatter.5.cloned.1.call-done = f32[8,128,128]{2,1,0:T(8,128)} async-done(((f32[8,1024,128]{2,1,0:T(8,128)}), f32[8,128,128]{2,1,0:T(8,128)}) %reduce-scatter.5.cloned.1.call-update) | async-done | bytes 524304 | tf_op jit(solution)/shard_map/reduce_scatter | solution.py:23
  242.6 4.1 convolution_bitcast_fusion.1
  246.8 8.4 %reduce-scatter.9.cloned.1.call-done = f32[128,1024]{1,0:T(8,128)} async-done(((f32[128,2048]{1,0:T(8,128)}), f32[128,1024]{1,0:T(8,128)}) %reduce-scatter.9.cloned.1.call-update) | async-done | bytes 524304 | tf_op jit(solution)/shard_map/reduce_scatter | solution.py:48
  255.2 1.2 multiply_reduce_fusion
  256.4 2.5 psum.14
  258.8 1.9 multiply_convert_fusion
  260.8 50.6 %all-gather.2.cloned.1.call-done = bf16[1024,1024]{1,0:T(8,128)(2,1)} async-done(((bf16[128,1024]{1,0:T(8,128)(2,1)}), bf16[1024,1024]{1,0:T(8,128)(2,1)}) %all-gather.2.cloned.1.call-update) | async-done | bytes 2097168 | tf_op jit(solution)/shard_map/all_gather | solution.py:55
  311.3 5.9 %fusion.40 = f32[1024,1024]{1,0:T(8,128)} fusion(bf16[1024,1024]{1,0:T(8,128)(2,1)} %all-gather.2.cloned.1.call-done, bf16[1024,1024]{1,0:T(8,128)(2,1)S(1)} %copy-done), kind=kOutput, calls=%fused_computation.51 | convolution fusion | flops 2147483648 | bytes 8388608 | tf_op jit(solution)/shard_map/dot_general | solution.py:54
  317.3 27.0 %all-reduce.2.cloned.1.call-done = f32[1024,1024]{1,0:T(8,128)} async-done(((f32[1024,1024]{1,0:T(8,128)}), f32[1024,1024]{1,0:T(8,128)}) %all-reduce.2.cloned.1.call-update) | async-done | bytes 4194320 | tf_op jit(solution)/shard_map/psum | solution.py:59
  344.3 7.5 %fusion.28 = f32[1024,1024]{1,0:T(8,128)} fusion(bf16[1024,1024]{1,0:T(8,128)(2,1)} %param.19, f32[1024,1024]{1,0:T(8,128)} %all-reduce.2.cloned.1.call-done), kind=kOutput, calls=%fused_computation.32 | convolution fusion | flops 2156920832 | bytes 10485760 | tf_op jit(solution)/shard_map/dot_general | solution.py:62
  351.8 89.8 %reduce-scatter.11.cloned.1.call-done = f32[128,1024]{1,0:T(8,128)} async-done(((f32[1024,1024]{1,0:T(8,128)}), f32[128,1024]{1,0:T(8,128)}) %reduce-scatter.11.cloned.1.call-update) | async-done | bytes 524304 | tf_op jit(solution)/shard_map/reduce_scatter | solution.py:61
  441.6 1.8 add_convert_fusion
  (50 shorter events, 7.2 us)
Async XLA Ops:
  6.5 304.8 %copy-start = (bf16[1024,1024]{1,0:T(8,128)(2,1)S(1)}, bf16[1024,1024]{1,0:T(8,128)(2,1)}, u32[]{:S(2)}) copy-start(bf16[1024,1024]{1,0:T(8,128)(2,1)} %param.18) | copy-start | bytes 6291460
  6.5 145.4 %reduce-scatter.7.cloned.1.call-start = ((), (), s32[]{:S(2)}) async-start(), calls=%async_computation.5 | async-start | bytes 36864 | tf_op jit(solution)/shard_map/reduce_scatter | solution.py:22
  101.0 141.6 %reduce-scatter.5.cloned.1.call-start = ((), (), s32[]{:S(2)}) async-start(), calls=%async_computation.4 | async-start | bytes 4718592 | tf_op jit(solution)/shard_map/reduce_scatter | solution.py:23
  105.2 149.9 %reduce-scatter.9.cloned.1.call-start = ((), (), s32[]{:S(2)}) async-start(), calls=%async_computation.6 | async-start | bytes 1572864 | tf_op jit(solution)/shard_map/reduce_scatter | solution.py:48
  242.6 12.6 %copy-start.2 = (bf16[128,1024]{1,0:T(8,128)(2,1)S(1)}, bf16[128,1024]{1,0:T(8,128)(2,1)}, u32[]{:S(2)}) copy-start(bf16[128,1024]{1,0:T(8,128)(2,1)} %param.15) | copy-start | bytes 786436
  242.6 16.3 %copy-start.3 = (f32[1024]{0:T(1024)S(1)}, f32[1024]{0:T(1024)}, u32[]{:S(2)}) copy-start(f32[1024]{0:T(1024)} %param.17) | copy-start | bytes 12292
  246.7 64.6 %all-gather.2.cloned.1.call-start = ((), (), s32[]{:S(2)}) async-start(), calls=%async_computation.7 | async-start | bytes 2359296 | tf_op jit(solution)/shard_map/all_gather | solution.py:55
  260.7 83.6 %all-reduce.2.cloned.1.call-start = ((), (), s32[]{:S(2)}) async-start(), calls=%async_computation.8 | async-start | bytes 8388608 | tf_op jit(solution)/shard_map/psum | solution.py:59
  317.3 124.4 %reduce-scatter.11.cloned.1.call-start = ((), (), s32[]{:S(2)}) async-start(), calls=%async_computation.9 | async-start | bytes 4718592 | tf_op jit(solution)/shard_map/reduce_scatter | solution.py:61
  351.8 89.9 %copy-start.1 = (f32[128,1024]{1,0:T(8,128)S(1)}, f32[128,1024]{1,0:T(8,128)}, u32[]{:S(2)}) copy-start(f32[128,1024]{1,0:T(8,128)} %reduce-scatter.9.cloned.1.call-done) | copy-start | bytes 1572868
Sparse Core Ops, SparseCore 0:
  101.1 50.8 reduce-scatter.6
  155.6 86.9 reduce-scatter.4
  246.9 8.2 reduce-scatter.8
  260.8 50.4 all-gather.1
  317.4 26.8 all-reduce.1
  351.9 89.6 reduce-scatter.10
where the time goes:
time: 451 us; the launch traced here: 450 us
  waiting for transfers between devices  313 us (69%)
  matrix products  49.5 us (11%)
  blocking collectives  41.3 us (9%)
  other arithmetic  19.6 us (4%)
  between operations  13.5 us (3%)
  local copies, waits for them, and re-layouts  7.08 us (2%)
  loops' own time  5.98 us (1%)
    reduce_scatter x1, waiting for transfers between devices, merged(): lax.psum_scatter(context * factor[..., None], 'hits', scatter_dimension=1...  90.6 us
    reduce_scatter x1, waiting for transfers between devices, shards(): lax.psum_scatter(jnp.dot(hidden, down_proj, preferred_element_type=jnp.fl...  89.8 us
    all_gather x1, waiting for transfers between devices, shards(): lax.all_gather(normed, 'hits', axis=0, tiled=True)  50.6 us
    reduce_scatter x1, waiting for transfers between devices, merged(): lax.psum_scatter(row_total * factor, 'hits', scatter_dimension=1, tiled=T...  46.7 us
    pmax x1, blocking collectives, merged(): row_best = lax.pmax(row_top, 'hits')  38.8 us
    psum x1, waiting for transfers between devices, shards(): summed_units = lax.psum(partial_units, 'heads')  27 us
    dot_general x8, matrix products, one_head(): jnp.dot(weights.astype(jnp.bfloat16), v_head, preferred_element_type=jnp....  20.5 us
    dot_general x8, matrix products, one_head(): lax.dot_general(q_head, k_head, (((1,), (1,)), ((), ())), preferred_eleme...  11.6 us
  transfers between devices with their start and end apart: 6, of which 6 were waited for; matrix products, arithmetic and copies ran while one was open for 1% of the time, Pallas kernels for 0%

commit v1 on v0

v1 whole, which is shorter than its diff:
```python
import functools
import math

import jax
import jax.numpy as jnp
from jax import lax
from jax.experimental import pallas as pl
from jax.experimental.pallas import tpu as pltpu
from jax.sharding import PartitionSpec as P

HD = 128
LANES = 128
MESH = pl.DeviceIdType.MESH
F32 = jnp.float32
BF16 = jnp.bfloat16


def kernel(
    n,
    bias_ref, q_ref, k_ref, v_ref, lat_ref, gain_ref, wo_hbm, wu_hbm, wd_hbm,
    out_ref,
    wo, wu, wd,
    att_out, att_own, att_in, att_z, acc,
    psend, precv, sqs, sqr, stream,
    x_in, pu_own, pu_in, dy_out, dy_in, down_own, dz_in,
    w_sem, ay_s, ay_r, az_s, az_r, p_s, p_r, xz_s, xz_r, xy_s, xy_r, u_s, u_r, dy_s, dy_r, dz_s, dz_r,
):
    me = lax.axis_index("hits")
    core = lax.axis_index("heads")
    z, y = me // 2, me % 2
    outer = n // 2
    partner = z * 2 + (1 - y)
    sibling = 1 - core
    rows, width = q_ref.shape
    blk = rows // n
    heads = width // HD
    scale = math.log2(math.e) / math.sqrt(HD)
    features = wo.shape[1]

    def peer(zz):
        return lax.rem(zz + 2 * outer, outer) * 2 + y

    barrier = pltpu.get_barrier_semaphore()
    pl.semaphore_signal(barrier, inc=1, device_id={"hits": partner}, device_id_type=MESH)
    pl.semaphore_signal(barrier, inc=1, device_id={"heads": sibling}, device_id_type=MESH)
    for k in range(1, outer):
        pl.semaphore_signal(barrier, inc=1, device_id={"hits": peer(z + k)}, device_id_type=MESH)

    weights = [
        pltpu.make_async_copy(src, dst, w_sem.at[i])
        for i, (src, dst) in enumerate(((wo_hbm, wo), (wu_hbm, wu), (wd_hbm, wd)))
    ]
    for w in weights:
        w.start()

    def to_hits(src, dst, s, r, where):
        return pltpu.make_async_remote_copy(
            src_ref=src, dst_ref=dst, send_sem=s, recv_sem=r,
            device_id={"hits": where}, device_id_type=MESH,
        )

    def to_sibling(src, dst, s, r):
        return pltpu.make_async_remote_copy(
            src_ref=src, dst_ref=dst, send_sem=s, recv_sem=r,
            device_id={"heads": sibling}, device_id_type=MESH,
        )

    group = max(outer // 2, 1)
    tall = group * blk
    lane = lax.broadcasted_iota(jnp.int32, (tall, LANES), 1)

    def attend(chunk, half, dest):
        starts = []
        for g in range(group):
            zz = lax.rem(z + 1 + chunk * group + g, outer)
            starts.append(pl.multiple_of((zz * 2 + half) * blk, blk))
        stats = jnp.zeros((tall, LANES), F32)
        for h in range(heads):
            cols = slice(h * HD, (h + 1) * HD)
            q = jnp.concatenate([q_ref[pl.ds(s, blk), cols] for s in starts], axis=0)
            s = lax.dot_general(
                q, k_ref[:, cols], (((1,), (1,)), ((), ())), preferred_element_type=F32
            )
            s = s + bias_ref[...]
            top = (jnp.max(s, axis=1, keepdims=True) * scale).astype(BF16).astype(F32)
            p = jnp.exp2(s * scale - top)
            total = jnp.sum(p, axis=1, keepdims=True)
            o = jnp.dot(p.astype(BF16), v_ref[:, cols], preferred_element_type=F32).astype(BF16)
            high = total.astype(BF16).astype(F32)
            stats = jnp.where(lane == h, top, stats)
            stats = jnp.where(lane == heads + h, high, stats)
            stats = jnp.where(lane == 2 * heads + h, total - high, stats)
            for g in range(group):
                dest[chunk * group + g, :, cols] = o[g * blk:(g + 1) * blk]
        st = stats.astype(BF16)
        for g in range(group):
            dest[chunk * group + g, :, width:] = st[g * blk:(g + 1) * blk]

    def att_y(j):
        return to_hits(att_out.at[j], att_in.at[j], ay_s.at[j], ay_r.at[j], partner)

    def att_zc(j):
        return to_hits(att_own.at[j], att_z.at[j], az_s.at[j], az_r.at[j], peer(z + 1 + j))

    @pl.loop(0, outer // group)
    def _(chunk):
        attend(chunk, 1 - y, att_out)

        @pl.when(chunk == 0)
        def _():
            pl.semaphore_wait(barrier, outer + 1)

        for g in range(group):
            att_y(chunk * group + g).start()

    @pl.loop(0, outer // group)
    def _(chunk):
        attend(chunk, y, att_own)

    small = lax.broadcasted_iota(jnp.int32, (blk, LANES), 1)

    def columns(stats, h):
        top = stats[:, h:h + 1]
        total = stats[:, heads + h:heads + h + 1] + stats[:, 2 * heads + h:2 * heads + h + 1]
        return top, total

    @pl.loop(0, outer)
    def _(j):
        att_y(j).wait_recv()
        a = att_own[j, :, width:].astype(F32)
        b = att_in[j, :, width:].astype(F32)
        stats = jnp.zeros((blk, LANES), F32)
        for h in range(heads):
            cols = slice(h * HD, (h + 1) * HD)
            ta, la = columns(a, h)
            tb, lb = columns(b, h)
            top = jnp.maximum(ta, tb)
            fa, fb = jnp.exp2(ta - top), jnp.exp2(tb - top)
            total = la * fa + lb * fb
            high = total.astype(BF16).astype(F32)
            stats = jnp.where(small == h, top, stats)
            stats = jnp.where(small == heads + h, high, stats)
            stats = jnp.where(small == 2 * heads + h, total - high, stats)
            o = att_own[j, :, cols].astype(F32) * fa + att_in[j, :, cols].astype(F32) * fb
            att_own[j, :, cols] = o.astype(BF16)
        att_own[j, :, width:] = stats.astype(BF16)

        @pl.when(j < outer - 1)
        def _():
            att_zc(j).start()

    @pl.loop(0, outer - 1)
    def _(j):
        att_zc(j).wait_recv()

    parts = [(att_own, outer - 1)] + [(att_z, j) for j in range(outer - 1)]
    stat = [ref[j, :, width:].astype(F32) for ref, j in parts]
    for h in range(heads):
        cols = slice(h * HD, (h + 1) * HD)
        pairs = [columns(s, h) for s in stat]
        top = functools.reduce(jnp.maximum, [t for t, _ in pairs])
        factors = [jnp.exp2(t - top) for t, _ in pairs]
        total = sum(l * f for (_, l), f in zip(pairs, factors))
        o = sum(ref[j, :, cols].astype(F32) * f for (ref, j), f in zip(parts, factors))
        acc[:, cols] = (o / total).astype(BF16)

    weights[0].wait()
    theirs = pl.ds(pl.multiple_of(sibling * width, width), width)
    ours = pl.ds(pl.multiple_of(core * width, width), width)
    psend[...] = jnp.dot(acc[...], wo[:, theirs], preferred_element_type=F32)
    proj = to_sibling(psend, precv, p_s.at[0], p_r.at[0])
    proj.start()
    stream[...] = lat_ref[...].astype(F32) + jnp.dot(acc[...], wo[:, ours], preferred_element_type=F32)
    proj.wait_recv()
    summed = stream[...] + precv[...]
    stream[...] = summed
    own_sq = jnp.sum(summed * summed, axis=1, keepdims=True)
    sqs[...] = jnp.broadcast_to(own_sq, sqs.shape)
    squares = to_sibling(sqs, sqr, p_s.at[1], p_r.at[1])
    squares.start()
    squares.wait_recv()
    factor = lax.rsqrt((sqs[:, :1] + sqr[:, :1]) / features + 1e-06)
    x_in[0, 0] = (stream[...] * factor * gain_ref[...]).astype(BF16)

    def x_y(k):
        return to_hits(x_in.at[k, 0], x_in.at[k, 1], xy_s.at[k], xy_r.at[k], partner)

    def x_z(k):
        return to_hits(x_in.at[0, 0], x_in.at[k, 0], xz_s.at[k], xz_r.at[k], peer(z + k))

    def units(k):
        return to_sibling(pu_own.at[k], pu_in.at[k], u_s.at[k], u_r.at[k])

    def down_y(k):
        return to_hits(dy_out.at[k], dy_in.at[k], dy_s.at[k], dy_r.at[k], partner)

    def down_z(k):
        return to_hits(down_own.at[k], dz_in.at[k], dz_s.at[k], dz_r.at[k], peer(z - k))

    x_y(0).start()

    @pl.loop(1, outer)
    def _(k):
        x_z(k).start()

    weights[1].wait()
    weights[2].wait()

    @pl.loop(0, outer + 2)
    def _(k):
        @pl.when(k < outer)
        def _():
            x_y(k).wait_recv()
            x = x_in[k].reshape(2 * blk, width)
            pu_own[k] = jnp.dot(x, wu[...], preferred_element_type=F32)
            units(k).start()

        @pl.when(k < outer - 1)
        def _():
            x_z(k + 1).wait_recv()
            x_y(k + 1).start()

        @pl.when((k >= 1) & (k <= outer))
        def _():
            units(k - 1).wait_recv()
            hidden = jax.nn.gelu(pu_own[k - 1] + pu_in[k - 1]).astype(BF16)
            d = jnp.dot(hidden, wd[...], preferred_element_type=F32).astype(BF16)
            dy_out[k - 1] = d[blk:]
            down_y(k - 1).start()
            down_own[k - 1] = d[:blk]

        @pl.when(k >= 2)
        def _():
            down_y(k - 2).wait_recv()
            both = down_own[k - 2].astype(F32) + dy_in[k - 2].astype(F32)

            @pl.when(k == 2)
            def _():
                stream[...] = stream[...] + both

            @pl.when(k > 2)
            def _():
                down_own[k - 2] = both.astype(BF16)
                down_z(k - 2).start()

    @pl.loop(1, outer)
    def _(k):
        down_z(k).wait_recv()
        stream[...] = stream[...] + dz_in[k].astype(F32)

    out_ref[...] = stream[...].astype(BF16)

    proj.wait_send()
    squares.wait_send()

    @pl.loop(0, outer)
    def _(k):
        att_y(k).wait_send()
        x_y(k).wait_send()
        units(k).wait_send()
        down_y(k).wait_send()

    @pl.loop(1, outer)
    def _(k):
        att_zc(k - 1).wait_send()
        x_z(k).wait_send()
        down_z(k).wait_send()


def shards(n, queries, keys, values, hit_counts, latents, out_proj, norm_gain, up_proj, down_proj):
    rows, width = queries.shape
    blk = rows // n
    outer = n // 2
    hidden = up_proj.shape[1]
    features = out_proj.shape[1]
    live = lax.broadcasted_iota(jnp.int32, (1, keys.shape[0]), 1) < hit_counts[0]
    bias = jnp.where(live, 0.0, -1e30).astype(F32)
    vmem = pl.BlockSpec(memory_space=pltpu.VMEM)
    hbm = pl.BlockSpec(memory_space=pl.ANY)
    wide = width + LANES
    dma = lambda m: pltpu.SemaphoreType.DMA((m,))
    return pl.pallas_call(
        functools.partial(kernel, n),
        out_shape=jax.ShapeDtypeStruct(latents.shape, BF16),
        in_specs=[vmem] * 6 + [hbm] * 3,
        out_specs=vmem,
        scratch_shapes=[
            pltpu.VMEM(out_proj.shape, BF16),
            pltpu.VMEM(up_proj.shape, BF16),
            pltpu.VMEM(down_proj.shape, BF16),
            pltpu.VMEM((outer, blk, wide), BF16),
            pltpu.VMEM((outer, blk, wide), BF16),
            pltpu.VMEM((outer, blk, wide), BF16),
            pltpu.VMEM((outer - 1, blk, wide), BF16),
            pltpu.VMEM((blk, width), BF16),
            pltpu.VMEM((blk, width), F32),
            pltpu.VMEM((blk, width), F32),
            pltpu.VMEM((blk, LANES), F32),
            pltpu.VMEM((blk, LANES), F32),
            pltpu.VMEM((blk, width), F32),
            pltpu.VMEM((outer, 2, blk, width), BF16),
            pltpu.VMEM((outer, 2 * blk, hidden), F32),
            pltpu.VMEM((outer, 2 * blk, hidden), F32),
            pltpu.VMEM((outer, blk, width), BF16),
            pltpu.VMEM((outer, blk, width), BF16),
            pltpu.VMEM((outer, blk, width), BF16),
            pltpu.VMEM((outer, blk, width), BF16),
            dma(3),
            dma(outer), dma(outer), dma(outer), dma(outer),
            dma(2), dma(2),
            dma(outer), dma(outer), dma(outer), dma(outer),
            dma(outer), dma(outer), dma(outer), dma(outer), dma(outer), dma(outer),
        ],
        compiler_params=pltpu.CompilerParams(
            collective_id=0, has_side_effects=True, vmem_limit_bytes=56 * 1024 * 1024
        ),
        cost_estimate=pl.CostEstimate(
            flops=4 * rows * keys.shape[0] * width + 2 * blk * width * features + 4 * rows * width * hidden,
            bytes_accessed=16 * 1024 * 1024,
            transcendentals=rows * keys.shape[0] * (width // HD),
        ),
    )(bias, queries, keys, values, latents, norm_gain[None, :], out_proj, up_proj, down_proj)


def solution(mesh):
    return jax.shard_map(
        functools.partial(shards, mesh.shape["hits"]),
        mesh=mesh,
        in_specs=(
            P("groups", "heads"),
            P(("groups", "hits"), "heads"),
            P(("groups", "hits"), "heads"),
            P(("groups", "hits")),
            P(("groups", "hits"), "heads"),
            P("heads", None),
            P("heads"),
            P("heads", "hits"),
            P("hits", "heads"),
        ),
        out_specs=P(("groups", "hits"), "heads"),
        check_vma=False,
    )
```

time: 451 us -> 127 us (0.28)
  waiting for transfers between devices: 313 us -> 0 us
  Pallas kernels: 0 us -> 124 us
  matrix products: 49.5 us -> 0 us
  blocking collectives: 41.3 us -> 0 us
  other arithmetic: 19.6 us -> 0.58 us
  between operations: 13.5 us -> 0.66 us
  loops' own time: 5.98 us -> 0 us
  local copies, waits for them, and re-layouts: 7.08 us -> 1.67 us
    reduce_scatter x4 -> x0, waiting for transfers between devices: 235 us -> none  [the longest x1 90.6 us: merged(): lax.psum_scatter(context * factor[..., None], 'hits', scatter_dimension=1...]
    pallas_call x0 -> x1, Pallas kernels: none -> 124 us  [shards(): pl.pallas_call(functools.partial(kernel, n), out_shape=jax.ShapeDtypeStru...]
    all_gather x1 -> x0, waiting for transfers between devices: 50.6 us -> none  [shards(): lax.all_gather(normed, 'hits', axis=0, tiled=True)]
    dot_general x19 -> x0, matrix products: 49.5 us -> none  [the longest x8 20.5 us: one_head(): jnp.dot(weights.astype(jnp.bfloat16), v_head, preferred_element_type=jnp....]
    pmax x1 -> x0, blocking collectives: 38.8 us -> none  [merged(): row_best = lax.pmax(row_top, 'hits')]
    psum x1 -> x0, waiting for transfers between devices: 27 us -> none  [shards(): summed_units = lax.psum(partial_units, 'heads')]
    another operation x1 -> x0, loops' own time: 5.98 us -> none  [shards(): lax.map(one_head, jnp.arange(local_heads, dtype=jnp.int32))]
    reduce_sum x9 -> x0, other arithmetic: 5.67 us -> none  [the longest x8 4.48 us: one_head(): row_total = jnp.sum(weights, axis=1)]
  transfers between devices with their start and end apart: 6 -> 0, of which waited for: 6 -> 0; matrix products, arithmetic and copies ran while one was open for 1% -> 0% of each run, Pallas kernels for 0% -> 0%
where the time goes in v1:
time: 127 us
  Pallas kernels  124 us (98%)
  local copies, waits for them, and re-layouts  1.67 us (1%)
    pallas_call x1, Pallas kernels, shards(): pl.pallas_call(functools.partial(kernel, n), out_shape=jax.ShapeDtypeStru...  124 us

profile of v1, /device:TPU:0, one launch (start us, length us, event | category | flops | bytes accessed | tf_op | source)
XLA Modules:
  0.0 126.6 jit_solution(10071897023800911855)
XLA Ops:
  0.7 0.6 compare_select_fusion.bias_ref
  1.2 123.7 %shard_map.91 = bf16[128,1024]{1,0:T(8,128)(2,1)} custom-call(f32[1,512]{1,0:T(1,128)} %compare_select_fusion.bias_ref, bf16[1024,1024]{1,0:T(8,128)(2,1)} %q_ref.1, bf16[512,1024]{1,0:T(8,128)(2,1)} %k_ref.1, bf16[512,1024]{1,0:T(8,128)(2,1)} %v_ref.1, bf16[128,1024]{1,0:T(8,128)(2,1)} %lat_ref.1, f32[1,1024]{1,0:T(1,128)} %bitcast.3, ...), custom_call_target="tpu_custom_call" | custom-call | flops 6979321856 | bytes 16777216 | tf_op jit(solution)/shard_map/pallas_call | solution.py:282
  124.9 1.7 %copy.12 = bf16[128,1024]{1,0:T(8,128)(2,1)} copy(bf16[128,1024]{1,0:T(8,128)(2,1)} %shard_map.91) | data formatting | bytes 524288

commit v2 on v1

--- a/solution.py
+++ b/solution.py
@@ -180,73 +180,114 @@
     squares.start()
     squares.wait_recv()
     factor = lax.rsqrt((sqs[:, :1] + sqr[:, :1]) / features + 1e-06)
-    x_in[0, 0] = (stream[...] * factor * gain_ref[...]).astype(BF16)
-
-    def x_y(k):
-        return to_hits(x_in.at[k, 0], x_in.at[k, 1], xy_s.at[k], xy_r.at[k], partner)
-
-    def x_z(k):
-        return to_hits(x_in.at[0, 0], x_in.at[k, 0], xz_s.at[k], xz_r.at[k], peer(z + k))
-
-    def units(k):
-        return to_sibling(pu_own.at[k], pu_in.at[k], u_s.at[k], u_r.at[k])
-
-    def down_y(k):
-        return to_hits(dy_out.at[k], dy_in.at[k], dy_s.at[k], dy_r.at[k], partner)
-
-    def down_z(k):
-        return to_hits(down_own.at[k], dz_in.at[k], dz_s.at[k], dz_r.at[k], peer(z - k))
-
-    x_y(0).start()
-
-    @pl.loop(1, outer)
-    def _(k):
-        x_z(k).start()
+    x_in[z, 0] = (stream[...] * factor * gain_ref[...]).astype(BF16)
+
+    last = outer - 1
+    near = jnp.minimum(z, last - z)
+    longer = jnp.where(2 * z < last, 1, -1)
+
+    def source(t):
+        paired = z + (2 * lax.rem(t, 2) - 1) * ((t + 1) // 2)
+        return jnp.where(t <= 2 * near, paired, z + longer * (t - near))
+
+    def x_y(zs):
+        return to_hits(x_in.at[zs, 0], x_in.at[zs, 1], xy_s.at[zs], xy_r.at[zs], partner)
+
+    def x_right(zs):
+        where = jnp.minimum(z + 1, last) * 2 + y
+        return to_hits(x_in.at[zs, 0], x_in.at[zs, 0], xz_s.at[0, zs], xz_r.at[zs], where)
+
+    def x_left(zs):
+        where = jnp.maximum(z - 1, 0) * 2 + y
+        return to_hits(x_in.at[zs, 0], x_in.at[zs, 0], xz_s.at[1, zs], xz_r.at[zs], where)
+
+    def units(t):
+        return to_sibling(pu_own.at[t], pu_in.at[t], u_s.at[t], u_r.at[t])
+
+    def down_y(zs):
+        return to_hits(dy_out.at[zs], dy_in.at[zs], dy_s.at[zs], dy_r.at[zs], partner)
+
+    def down_z(zs):
+        return to_hits(down_own.at[zs], dz_in.at[z], dz_s.at[zs], dz_r.at[z], zs * 2 + y)
+
+    x_y(z).start()
+
+    @pl.when(z < last)
+    def _():
+        x_right(z).start()
+
+    @pl.when(z > 0)
+    def _():
+        x_left(z).start()
 
     weights[1].wait()
     weights[2].wait()
 
     @pl.loop(0, outer + 2)
-    def _(k):
-        @pl.when(k < outer)
-        def _():
-            x_y(k).wait_recv()
-            x = x_in[k].reshape(2 * blk, width)
-            pu_own[k] = jnp.dot(x, wu[...], preferred_element_type=F32)
-            units(k).start()
-
-        @pl.when(k < outer - 1)
-        def _():
-            x_z(k + 1).wait_recv()
-            x_y(k + 1).start()
-
-        @pl.when((k >= 1) & (k <= outer))
-        def _():
-            units(k - 1).wait_recv()
-            hidden = jax.nn.gelu(pu_own[k - 1] + pu_in[k - 1]).astype(BF16)
+    def _(t):
+        @pl.when(t < outer)
+        def _():
+            zs = source(t)
+            x_y(zs).wait_recv()
+            x = x_in[zs].reshape(2 * blk, width)
+            pu_own[t] = jnp.dot(x, wu[...], preferred_element_type=F32)
+            units(t).start()
+
+        @pl.when(z - t - 1 >= 0)
+        def _():
+            zs = z - t - 1
+            x_right(zs).wait_recv()
+
+            @pl.when(z < last)
+            def _():
+                x_right(zs).start()
+
+        @pl.when(z + t + 1 <= last)
+        def _():
+            zs = z + t + 1
+            x_left(zs).wait_recv()
+
+            @pl.when(z > 0)
+            def _():
+                x_left(zs).start()
+
+        @pl.when(t < last)
+        def _():
+            x_y(source(t + 1)).start()
+
+        @pl.when((t >= 1) & (t <= outer))
+        def _():
+            zs = source(t - 1)
+            units(t - 1).wait_recv()
+            hidden = jax.nn.gelu(pu_own[t - 1] + pu_in[t - 1]).astype(BF16)
             d = jnp.dot(hidden, wd[...], preferred_element_type=F32).astype(BF16)
-            dy_out[k - 1] = d[blk:]
-            down_y(k - 1).start()
-            down_own[k - 1] = d[:blk]
-
-        @pl.when(k >= 2)
-        def _():
-            down_y(k - 2).wait_recv()
-            both = down_own[k - 2].astype(F32) + dy_in[k - 2].astype(F32)
-
-            @pl.when(k == 2)
+            dy_out[zs] = d[blk:]
+            down_own[zs] = d[:blk]
+
+            @pl.when(t > 1)
             def _():
-                stream[...] = stream[...] + both
-
-            @pl.when(k > 2)
+                down_y(zs).start()
+
+            @pl.when(t == outer)
             def _():
-                down_own[k - 2] = both.astype(BF16)
-                down_z(k - 2).start()
+                down_y(z).start()
+
+        @pl.when(t > 2)
+        def _():
+            zs = source(t - 2)
+            down_y(zs).wait_recv()
+            both = down_own[zs].astype(F32) + dy_in[zs].astype(F32)
+            down_own[zs] = both.astype(BF16)
+            down_z(zs).start()
+
+    down_y(z).wait_recv()
+    stream[...] = stream[...] + down_own[z].astype(F32) + dy_in[z].astype(F32)
 
     @pl.loop(1, outer)
-    def _(k):
-        down_z(k).wait_recv()
-        stream[...] = stream[...] + dz_in[k].astype(F32)
+    def _(t):
+        zs = source(t)
+        to_hits(down_own.at[zs], dz_in.at[zs], dz_s.at[zs], dz_r.at[zs], zs * 2 + y).wait_recv()
+        stream[...] = stream[...] + dz_in[zs].astype(F32)
 
     out_ref[...] = stream[...].astype(BF16)
 
@@ -254,17 +295,27 @@
     squares.wait_send()
 
     @pl.loop(0, outer)
-    def _(k):
-        att_y(k).wait_send()
-        x_y(k).wait_send()
-        units(k).wait_send()
-        down_y(k).wait_send()
-
-    @pl.loop(1, outer)
-    def _(k):
-        att_zc(k - 1).wait_send()
-        x_z(k).wait_send()
-        down_z(k).wait_send()
+    def _(t):
+        att_y(t).wait_send()
+        x_y(t).wait_send()
+        units(t).wait_send()
+        down_y(t).wait_send()
+
+        @pl.when(t != z)
+        def _():
+            down_z(t).wait_send()
+
+        @pl.when((t <= z) & (z < last))
+        def _():
+            x_right(t).wait_send()
+
+        @pl.when((t >= z) & (z > 0))
+        def _():
+            x_left(t).wait_send()
+
+    @pl.loop(0, last)
+    def _(j):
+        att_zc(j).wait_send()
 
 
 def shards(n, queries, keys, values, hit_counts, latents, out_proj, norm_gain, up_proj, down_proj):
@@ -308,7 +359,7 @@
             dma(3),
             dma(outer), dma(outer), dma(outer), dma(outer),
             dma(2), dma(2),
-            dma(outer), dma(outer), dma(outer), dma(outer),
+            pltpu.SemaphoreType.DMA((2, outer)), dma(outer), dma(outer), dma(outer),
             dma(outer), dma(outer), dma(outer), dma(outer), dma(outer), dma(outer),
         ],
         compiler_params=pltpu.CompilerParams(

time: 127 us -> 114 us (0.90)
  Pallas kernels: 124 us -> 111 us
    pallas_call x1, Pallas kernels: 124 us -> 111 us  [shards(): pl.pallas_call(functools.partial(kernel, n), out_shape=jax.ShapeDtypeStru...]
where the time goes in v2:
time: 114 us
  Pallas kernels  111 us (97%)
  local copies, waits for them, and re-layouts  1.67 us (1%)
    pallas_call x1, Pallas kernels, shards(): pl.pallas_call(functools.partial(kernel, n), out_shape=jax.ShapeDtypeStru...  111 us

profile of v2, /device:TPU:0, one launch (start us, length us, event | category | flops | bytes accessed | tf_op | source)
XLA Modules:
  0.0 114.2 jit_solution(2172637662376262781)
XLA Ops:
  0.7 0.6 compare_select_fusion.bias_ref
  1.2 111.3 %shard_map.91 = bf16[128,1024]{1,0:T(8,128)(2,1)} custom-call(f32[1,512]{1,0:T(1,128)} %compare_select_fusion.bias_ref, bf16[1024,1024]{1,0:T(8,128)(2,1)} %q_ref.1, bf16[512,1024]{1,0:T(8,128)(2,1)} %k_ref.1, bf16[512,1024]{1,0:T(8,128)(2,1)} %v_ref.1, bf16[128,1024]{1,0:T(8,128)(2,1)} %lat_ref.1, f32[1,1024]{1,0:T(1,128)} %bitcast.3, ...), custom_call_target="tpu_custom_call" | custom-call | flops 6979321856 | bytes 16777216 | tf_op jit(solution)/shard_map/pallas_call | solution.py:333
  112.5 1.7 %copy.12 = bf16[128,1024]{1,0:T(8,128)(2,1)} copy(bf16[128,1024]{1,0:T(8,128)(2,1)} %shard_map.91) | data formatting | bytes 524288

commit v3 on v2

--- a/solution.py
+++ b/solution.py
@@ -20,10 +20,10 @@
     bias_ref, q_ref, k_ref, v_ref, lat_ref, gain_ref, wo_hbm, wu_hbm, wd_hbm,
     out_ref,
     wo, wu, wd,
-    att_out, att_own, att_in, att_z, acc,
+    att_out, att_own, att_in, att_z, st_out, st_own, st_in, st_z, acc,
     psend, precv, sqs, sqr, stream,
     x_in, pu_own, pu_in, dy_out, dy_in, down_own, dz_in,
-    w_sem, ay_s, ay_r, az_s, az_r, p_s, p_r, xz_s, xz_r, xy_s, xy_r, u_s, u_r, dy_s, dy_r, dz_s, dz_r,
+    w_sem, ay_s, ay_r, az_s, az_r, sy_s, sy_r, sz_s, sz_r, p_s, p_r, xz_s, xz_r, xy_s, xy_r, u_s, u_r, dy_s, dy_r, dz_s, dz_r,
 ):
     me = lax.axis_index("hits")
     core = lax.axis_index("heads")
@@ -65,15 +65,21 @@
             device_id={"heads": sibling}, device_id_type=MESH,
         )
 
+    last = outer - 1
+    near = jnp.minimum(z, last - z)
+    longer = jnp.where(2 * z < last, 1, -1)
+
+    def source(t):
+        paired = z + (2 * lax.rem(t, 2) - 1) * ((t + 1) // 2)
+        return jnp.where(t <= 2 * near, paired, z + longer * (t - near))
+
     group = max(outer // 2, 1)
     tall = group * blk
     lane = lax.broadcasted_iota(jnp.int32, (tall, LANES), 1)
 
-    def attend(chunk, half, dest):
-        starts = []
-        for g in range(group):
-            zz = lax.rem(z + 1 + chunk * group + g, outer)
-            starts.append(pl.multiple_of((zz * 2 + half) * blk, blk))
+    def attend(chunk, half, dest, stat_dest):
+        owners = [source(last - (chunk * group + g)) for g in range(group)]
+        starts = [pl.multiple_of((zz * 2 + half) * blk, blk) for zz in owners]
         stats = jnp.zeros((tall, LANES), F32)
         for h in range(heads):
             cols = slice(h * HD, (h + 1) * HD)
@@ -82,87 +88,88 @@
                 q, k_ref[:, cols], (((1,), (1,)), ((), ())), preferred_element_type=F32
             )
             s = s + bias_ref[...]
-            top = (jnp.max(s, axis=1, keepdims=True) * scale).astype(BF16).astype(F32)
+            top = jnp.max(s, axis=1, keepdims=True) * scale
             p = jnp.exp2(s * scale - top)
             total = jnp.sum(p, axis=1, keepdims=True)
             o = jnp.dot(p.astype(BF16), v_ref[:, cols], preferred_element_type=F32).astype(BF16)
-            high = total.astype(BF16).astype(F32)
             stats = jnp.where(lane == h, top, stats)
-            stats = jnp.where(lane == heads + h, high, stats)
-            stats = jnp.where(lane == 2 * heads + h, total - high, stats)
+            stats = jnp.where(lane == heads + h, total, stats)
             for g in range(group):
-                dest[chunk * group + g, :, cols] = o[g * blk:(g + 1) * blk]
-        st = stats.astype(BF16)
+                dest[owners[g], :, cols] = o[g * blk:(g + 1) * blk]
         for g in range(group):
-            dest[chunk * group + g, :, width:] = st[g * blk:(g + 1) * blk]
-
-    def att_y(j):
-        return to_hits(att_out.at[j], att_in.at[j], ay_s.at[j], ay_r.at[j], partner)
-
-    def att_zc(j):
-        return to_hits(att_own.at[j], att_z.at[j], az_s.at[j], az_r.at[j], peer(z + 1 + j))
+            stat_dest[owners[g]] = stats[g * blk:(g + 1) * blk].T[:2 * heads]
+
+    def att_y(d):
+        return (
+            to_hits(st_out.at[d], st_in.at[d], sy_s.at[d], sy_r.at[d], partner),
+            to_hits(att_out.at[d], att_in.at[d], ay_s.at[d], ay_r.at[d], partner),
+        )
+
+    def att_z_step(side, d):
+        zz = jnp.minimum(z + 1, last) if side == 0 else jnp.maximum(z - 1, 0)
+        where = zz * 2 + y
+        return (
+            to_hits(st_own.at[d], st_z.at[side, d], sz_s.at[d], sz_r.at[side, d], where),
+            to_hits(att_own.at[d], att_z.at[side, d], az_s.at[d], az_r.at[side, d], where),
+        )
 
     @pl.loop(0, outer // group)
     def _(chunk):
-        attend(chunk, 1 - y, att_out)
+        attend(chunk, 1 - y, att_out, st_out)
 
         @pl.when(chunk == 0)
         def _():
             pl.semaphore_wait(barrier, outer + 1)
 
         for g in range(group):
-            att_y(chunk * group + g).start()
+            for c in att_y(source(last - (chunk * group + g))):
+                c.start()
 
     @pl.loop(0, outer // group)
     def _(chunk):
-        attend(chunk, y, att_own)
-
-    small = lax.broadcasted_iota(jnp.int32, (blk, LANES), 1)
-
-    def columns(stats, h):
-        top = stats[:, h:h + 1]
-        total = stats[:, heads + h:heads + h + 1] + stats[:, 2 * heads + h:2 * heads + h + 1]
-        return top, total
+        attend(chunk, y, att_own, st_own)
+
+    def spread(rows_of):
+        pad = jnp.zeros((LANES - sum(r.shape[0] for r in rows_of), blk), F32)
+        return jnp.concatenate(rows_of + [pad], axis=0).T
+
+    def merge(d, values, stats):
+        a, b = st_own[d], stats
+        ta, la, tb, lb = a[:heads], a[heads:], b[:heads], b[heads:]
+        top = jnp.maximum(ta, tb)
+        fa, fb = jnp.exp2(ta - top), jnp.exp2(tb - top)
+        st_own[d] = jnp.concatenate([top, la * fa + lb * fb], axis=0)
+        f = spread([fa, fb])
+        for h in range(heads):
+            cols = slice(h * HD, (h + 1) * HD)
+            o = att_own[d, :, cols].astype(F32) * f[:, h:h + 1]
+            o = o + values[:, cols].astype(F32) * f[:, heads + h:heads + h + 1]
+            att_own[d, :, cols] = o.astype(BF16)
 
     @pl.loop(0, outer)
     def _(j):
-        att_y(j).wait_recv()
-        a = att_own[j, :, width:].astype(F32)
-        b = att_in[j, :, width:].astype(F32)
-        stats = jnp.zeros((blk, LANES), F32)
-        for h in range(heads):
-            cols = slice(h * HD, (h + 1) * HD)
-            ta, la = columns(a, h)
-            tb, lb = columns(b, h)
-            top = jnp.maximum(ta, tb)
-            fa, fb = jnp.exp2(ta - top), jnp.exp2(tb - top)
-            total = la * fa + lb * fb
-            high = total.astype(BF16).astype(F32)
-            stats = jnp.where(small == h, top, stats)
-            stats = jnp.where(small == heads + h, high, stats)
-            stats = jnp.where(small == 2 * heads + h, total - high, stats)
-            o = att_own[j, :, cols].astype(F32) * fa + att_in[j, :, cols].astype(F32) * fb
-            att_own[j, :, cols] = o.astype(BF16)
-        att_own[j, :, width:] = stats.astype(BF16)
-
-        @pl.when(j < outer - 1)
-        def _():
-            att_zc(j).start()
-
-    @pl.loop(0, outer - 1)
-    def _(j):
-        att_zc(j).wait_recv()
-
-    parts = [(att_own, outer - 1)] + [(att_z, j) for j in range(outer - 1)]
-    stat = [ref[j, :, width:].astype(F32) for ref, j in parts]
+        d = source(last - j)
+        for c in att_y(d):
+            c.wait_recv()
+        merge(d, att_in.at[d], st_in[d])
+
+        for side, arrives in ((0, (d >= z) & (z > 0)), (1, (d <= z) & (z < last))):
+            @pl.when(arrives)
+            def _():
+                for c in att_z_step(side, d):
+                    c.wait_recv()
+                merge(d, att_z.at[side, d], st_z[side, d])
+
+        for side, leaves in ((0, d > z), (1, d < z)):
+            @pl.when(leaves)
+            def _():
+                for c in att_z_step(side, d):
+                    c.start()
+
+    inverse = spread([1.0 / st_own[z][heads:]])
     for h in range(heads):
         cols = slice(h * HD, (h + 1) * HD)
-        pairs = [columns(s, h) for s in stat]
-        top = functools.reduce(jnp.maximum, [t for t, _ in pairs])
-        factors = [jnp.exp2(t - top) for t, _ in pairs]
-        total = sum(l * f for (_, l), f in zip(pairs, factors))
-        o = sum(ref[j, :, cols].astype(F32) * f for (ref, j), f in zip(parts, factors))
-        acc[:, cols] = (o / total).astype(BF16)
+        acc[:, cols] = (att_own[z, :, cols].astype(F32) * inverse[:, h:h + 1]).astype(BF16)
 
     weights[0].wait()
     theirs = pl.ds(pl.multiple_of(sibling * width, width), width)
@@ -182,14 +189,6 @@
     factor = lax.rsqrt((sqs[:, :1] + sqr[:, :1]) / features + 1e-06)
     x_in[z, 0] = (stream[...] * factor * gain_ref[...]).astype(BF16)
 
-    last = outer - 1
-    near = jnp.minimum(z, last - z)
-    longer = jnp.where(2 * z < last, 1, -1)
-
-    def source(t):
-        paired = z + (2 * lax.rem(t, 2) - 1) * ((t + 1) // 2)
-        return jnp.where(t <= 2 * near, paired, z + longer * (t - near))
-
     def x_y(zs):
         return to_hits(x_in.at[zs, 0], x_in.at[zs, 1], xy_s.at[zs], xy_r.at[zs], partner)
 
@@ -296,7 +295,9 @@
 
     @pl.loop(0, outer)
     def _(t):
-        att_y(t).wait_send()
+        for c in att_y(t):
+            c.wait_send()
+
         x_y(t).wait_send()
         units(t).wait_send()
         down_y(t).wait_send()
@@ -304,6 +305,8 @@
         @pl.when(t != z)
         def _():
             down_z(t).wait_send()
+            for c in att_z_step(0, t):
+                c.wait_send()
 
         @pl.when((t <= z) & (z < last))
         def _():
@@ -312,10 +315,6 @@
         @pl.when((t >= z) & (z > 0))
         def _():
             x_left(t).wait_send()
-
-    @pl.loop(0, last)
-    def _(j):
-        att_zc(j).wait_send()
 
 
 def shards(n, queries, keys, values, hit_counts, latents, out_proj, norm_gain, up_proj, down_proj):
@@ -328,7 +327,7 @@
     bias = jnp.where(live, 0.0, -1e30).astype(F32)
     vmem = pl.BlockSpec(memory_space=pltpu.VMEM)
     hbm = pl.BlockSpec(memory_space=pl.ANY)
-    wide = width + LANES
+    heads = width // HD
     dma = lambda m: pltpu.SemaphoreType.DMA((m,))
     return pl.pallas_call(
         functools.partial(kernel, n),
@@ -339,10 +338,14 @@
             pltpu.VMEM(out_proj.shape, BF16),
             pltpu.VMEM(up_proj.shape, BF16),
             pltpu.VMEM(down_proj.shape, BF16),
-            pltpu.VMEM((outer, blk, wide), BF16),
-            pltpu.VMEM((outer, blk, wide), BF16),
-            pltpu.VMEM((outer, blk, wide), BF16),
-            pltpu.VMEM((outer - 1, blk, wide), BF16),
+            pltpu.VMEM((outer, blk, width), BF16),
+            pltpu.VMEM((outer, blk, width), BF16),
+            pltpu.VMEM((outer, blk, width), BF16),
+            pltpu.VMEM((2, outer, blk, width), BF16),
+            pltpu.VMEM((outer, 2 * heads, blk), F32),
+            pltpu.VMEM((outer, 2 * heads, blk), F32),
+            pltpu.VMEM((outer, 2 * heads, blk), F32),
+            pltpu.VMEM((2, outer, 2 * heads, blk), F32),
             pltpu.VMEM((blk, width), BF16),
             pltpu.VMEM((blk, width), F32),
             pltpu.VMEM((blk, width), F32),
@@ -357,7 +360,8 @@
             pltpu.VMEM((outer, blk, width), BF16),
             pltpu.VMEM((outer, blk, width), BF16),
             dma(3),
-            dma(outer), dma(outer), dma(outer), dma(outer),
+            dma(outer), dma(outer), dma(outer), pltpu.SemaphoreType.DMA((2, outer)),
+            dma(outer), dma(outer), dma(outer), pltpu.SemaphoreType.DMA((2, outer)),
             dma(2), dma(2),
             pltpu.SemaphoreType.DMA((2, outer)), dma(outer), dma(outer), dma(outer),
             dma(outer), dma(outer), dma(outer), dma(outer), dma(outer), dma(outer),

time: 114 us -> 107 us (0.939)
  Pallas kernels: 111 us -> 104 us
    pallas_call x1, Pallas kernels: 111 us -> 104 us  [shards(): pl.pallas_call(functools.partial(kernel, n), out_shape=jax.ShapeDtypeStru...]
where the time goes in v3:
time: 107 us
  Pallas kernels  104 us (97%)
  local copies, waits for them, and re-layouts  1.67 us (2%)
    pallas_call x1, Pallas kernels, shards(): pl.pallas_call(functools.partial(kernel, n), out_shape=jax.ShapeDtypeStru...  104 us

profile of v3, /device:TPU:0, one launch (start us, length us, event | category | flops | bytes accessed | tf_op | source)
XLA Modules:
  0.0 106.8 jit_solution(1379463973403956522)
XLA Ops:
  0.7 0.6 compare_select_fusion.bias_ref
  1.2 103.8 %shard_map.91 = bf16[128,1024]{1,0:T(8,128)(2,1)} custom-call(f32[1,512]{1,0:T(1,128)} %compare_select_fusion.bias_ref, bf16[1024,1024]{1,0:T(8,128)(2,1)} %q_ref.1, bf16[512,1024]{1,0:T(8,128)(2,1)} %k_ref.1, bf16[512,1024]{1,0:T(8,128)(2,1)} %v_ref.1, bf16[128,1024]{1,0:T(8,128)(2,1)} %lat_ref.1, f32[1,1024]{1,0:T(1,128)} %bitcast.3, ...), custom_call_target="tpu_custom_call" | custom-call | flops 6979321856 | bytes 16777216 | tf_op jit(solution)/shard_map/pallas_call | solution.py:332
  105.1 1.7 %copy.12 = bf16[128,1024]{1,0:T(8,128)(2,1)} copy(bf16[128,1024]{1,0:T(8,128)(2,1)} %shard_map.91) | data formatting | bytes 524288

commit v4 on v3

--- a/solution.py
+++ b/solution.py
@@ -224,6 +224,28 @@
 
     @pl.loop(0, outer + 2)
     def _(t):
+        @pl.when(z - t - 1 >= 0)
+        def _():
+            zs = z - t - 1
+            x_right(zs).wait_recv()
+
+            @pl.when(z < last)
+            def _():
+                x_right(zs).start()
+
+        @pl.when(z + t + 1 <= last)
+        def _():
+            zs = z + t + 1
+            x_left(zs).wait_recv()
+
+            @pl.when(z > 0)
+            def _():
+                x_left(zs).start()
+
+        @pl.when(t < last)
+        def _():
+            x_y(source(t + 1)).start()
+
         @pl.when(t < outer)
         def _():
             zs = source(t)
@@ -232,36 +254,12 @@
             pu_own[t] = jnp.dot(x, wu[...], preferred_element_type=F32)
             units(t).start()
 
-        @pl.when(z - t - 1 >= 0)
-        def _():
-            zs = z - t - 1
-            x_right(zs).wait_recv()
-
-            @pl.when(z < last)
-            def _():
-                x_right(zs).start()
-
-        @pl.when(z + t + 1 <= last)
-        def _():
-            zs = z + t + 1
-            x_left(zs).wait_recv()
-
-            @pl.when(z > 0)
-            def _():
-                x_left(zs).start()
-
-        @pl.when(t < last)
-        def _():
-            x_y(source(t + 1)).start()
-
         @pl.when((t >= 1) & (t <= outer))
         def _():
             zs = source(t - 1)
             units(t - 1).wait_recv()
             hidden = jax.nn.gelu(pu_own[t - 1] + pu_in[t - 1]).astype(BF16)
-            d = jnp.dot(hidden, wd[...], preferred_element_type=F32).astype(BF16)
-            dy_out[zs] = d[blk:]
-            down_own[zs] = d[:blk]
+            dy_out[zs] = jnp.dot(hidden[blk:], wd[...], preferred_element_type=F32).astype(BF16)
 
             @pl.when(t > 1)
             def _():
@@ -270,6 +268,8 @@
             @pl.when(t == outer)
             def _():
                 down_y(z).start()
+
+            down_own[zs] = jnp.dot(hidden[:blk], wd[...], preferred_element_type=F32).astype(BF16)
 
         @pl.when(t > 2)
         def _():

time: 107 us -> 107 us (level)
  no operation moved by 1% of the time
where the time goes in v4:
time: 107 us
  Pallas kernels  104 us (97%)
  local copies, waits for them, and re-layouts  1.67 us (2%)
    pallas_call x1, Pallas kernels, shards(): pl.pallas_call(functools.partial(kernel, n), out_shape=jax.ShapeDtypeStru...  104 us

profile of v4, /device:TPU:0, one launch (start us, length us, event | category | flops | bytes accessed | tf_op | source)
XLA Modules:
  0.0 106.6 jit_solution(3610836026833188746)
XLA Ops:
  0.7 0.6 compare_select_fusion.bias_ref
  1.2 103.7 %shard_map.91 = bf16[128,1024]{1,0:T(8,128)(2,1)} custom-call(f32[1,512]{1,0:T(1,128)} %compare_select_fusion.bias_ref, bf16[1024,1024]{1,0:T(8,128)(2,1)} %q_ref.1, bf16[512,1024]{1,0:T(8,128)(2,1)} %k_ref.1, bf16[512,1024]{1,0:T(8,128)(2,1)} %v_ref.1, bf16[128,1024]{1,0:T(8,128)(2,1)} %lat_ref.1, f32[1,1024]{1,0:T(1,128)} %bitcast.3, ...), custom_call_target="tpu_custom_call" | custom-call | flops 6979321856 | bytes 16777216 | tf_op jit(solution)/shard_map/pallas_call | solution.py:332
  104.9 1.7 %copy.12 = bf16[128,1024]{1,0:T(8,128)(2,1)} copy(bf16[128,1024]{1,0:T(8,128)(2,1)} %shard_map.91) | data formatting | bytes 524288
